TPU v7x, 128 devices: a whole 4x4x4 slice. The times are simulated.
128 devices in a mesh: group: 8 (over z, y_lo), proc: 16 (over x, y_hi, core).
Axes of the slice: x: 4, y: 4 (y_hi: 2, y_lo: 2; y = y_hi * 2 + y_lo), z: 4, core: 2. Of those that a mesh axis runs over, the one named last changes fastest.
Arguments:
- pattern: int32 [34], replicated, may hold values 0 or 1
- inverse_root: float32 [2, 768, 768], P(None, 'proc'), may hold values from -1.5 to 1.5, as said below
- inverse_one: float32 [2, 768, 1536], P(None, 'proc', 'group'), may hold values from -1.5 to 1.5, as said below
- inverse_two: float32 [2, 768, 3072], P(None, 'proc', 'group'), may hold values from -1.5 to 1.5, as said below
- inverse_three: float32 [2, 768, 6144], P(None, 'proc', 'group'), may hold values from -1.5 to 1.5, as said below
- lower_one: float32 [2, 1, 768, 1536], P(None, None, 'proc', 'group'), may hold values from -0.15625 to 0.15625
- lower_two: float32 [2, 2, 768, 3072], P(None, None, 'proc', 'group'), may hold values from -0.15625 to 0.15625
- lower_three: float32 [2, 3, 768, 6144], P(None, None, 'proc', 'group'), may hold values from -0.15625 to 0.15625
Outputs:
- upper_one: float32 [2, 1, 768, 1536], P(None, None, 'proc', 'group')
- upper_two: float32 [2, 2, 768, 3072], P(None, None, 'proc', 'group')
- upper_three: float32 [2, 3, 768, 6144], P(None, None, 'proc', 'group')
- diagonal_one: float32 [2, 768, 1536], P(None, 'proc', 'group')
- diagonal_two: float32 [2, 768, 3072], P(None, 'proc', 'group')
- diagonal_three: float32 [2, 768, 6144], P(None, 'proc', 'group')
Inputs may be any that keep to these rules, and one draw needn't show every extreme that they name: `inverse_root`: each 768 by 768 block along the last dimension is symmetric in both parts. `inverse_one`: each 768 by 768 block along the last dimension is symmetric in both parts. `inverse_two`: each 768 by 768 block along the last dimension is symmetric in both parts. `inverse_three`: each 768 by 768 block along the last dimension is symmetric in both parts.
All inputs are finite; a program needn't handle non-finite values.
Results may differ from a plain program's by a relative error of at most 0.0002.
Values sent between devices are 32-bit elements; how exact they have to be, the bound alone decides.
A program may use at most 128 MiB of HBM per device.

v0:
```python
import jax
import jax.numpy as jnp
from jax import lax
from jax.experimental import pallas as pl
from jax.experimental.pallas import tpu as pltpu
from jax.sharding import PartitionSpec as P

MESH = pl.DeviceIdType.MESH
S = 768
PROCS = 16
ROWS = S // PROCS
HALF = ROWS // 2
CHUNKS = 3
WIDTH = S // CHUNKS
WIDE = (256, 384)
COLS = (192, 384)
ROLES = 32


def split(value):
    high = value.astype(jnp.bfloat16)
    low = (value - high.astype(jnp.float32)).astype(jnp.bfloat16)
    return high, low


def dot(first, second):
    return jnp.dot(first, second, preferred_element_type=jnp.float32)


def complex_rows(high, low, real_high, real_low, imag_high, imag_low):
    both = high.shape[0]
    half = both // 2
    stacked = jnp.concatenate([high, low], axis=0)
    by_real = dot(stacked, real_high)
    by_real = by_real[:both] + by_real[both:] + dot(high, real_low)
    by_imag = dot(stacked, imag_high)
    by_imag = by_imag[:both] + by_imag[both:] + dot(high, imag_low)
    return by_real[:half] - by_imag[half:], by_imag[:half] + by_real[half:]


def kernel(
    pattern,
    inverse_root,
    inverse_one,
    inverse_two,
    inverse_three,
    lower_one,
    lower_two,
    lower_three,
    upper_one,
    upper_two,
    upper_three,
    diagonal_one,
    diagonal_two,
    diagonal_three,
    full_one,
    full_two,
    full_three,
    high_one,
    high_two,
    high_three,
    low_one,
    low_two,
    low_three,
    chain,
    join_one,
    join_two,
    joined,
    join_diag_one,
    join_diag_two,
    send_one,
    send_two,
    send_three,
    turned_one,
    turned_two,
    turned_three,
    gather_send,
    gather_recv,
    join_send,
    join_recv,
    turn_send,
    turn_recv,
):
    group = lax.axis_index("group")
    me = lax.axis_index("proc")
    x_at = me // 4
    y_at = me // 2 % 2
    core = me % 2

    def proc_of(dx, dy, dc=0):
        return lax.rem(x_at + dx, 4) * 4 + lax.rem(y_at + dy, 2) * 2 + lax.rem(core + dc, 2)

    right, left = proc_of(1, 0), proc_of(3, 0)
    far, pair, sibling = proc_of(2, 0), proc_of(0, 1), proc_of(0, 0, 1)
    pair_right, pair_left, pair_far = proc_of(1, 1), proc_of(3, 1), proc_of(2, 1)

    barrier = pltpu.get_barrier_semaphore()
    for step in range(1, PROCS):
        pl.semaphore_signal(
            barrier, inc=1, device_id=(group, lax.rem(me + step, PROCS)), device_id_type=MESH
        )
    for flip in range(1, 4):
        pl.semaphore_signal(barrier, inc=1, device_id=(group ^ flip, me), device_id_type=MESH)

    def keep(level, a):
        node = group // 2 ** (3 - level)
        first = (level - 2) * 2**level + 2
        return pattern[first + node * level + a].astype(jnp.float32)

    buffers = [full_one, full_two] + [full_three.at[c] for c in range(CHUNKS)]
    highs = [high_one, high_two] + [high_three.at[c] for c in range(CHUNKS)]
    lows = [low_one, low_two] + [low_three.at[c] for c in range(CHUNKS)]

    def rows_of(proc, offset=0):
        return pl.multiple_of(proc * ROWS + offset, 8)

    own = pl.ds(rows_of(me), ROWS)
    full_one[:, :, own, :] = jnp.zeros((2, 1, ROWS, WIDE[0]), jnp.float32)
    full_one[:, 0, own, : COLS[0]] = lower_one[:, 0] * keep(1, 0)
    for a in range(2):
        full_two[:, a, own, :] = lower_two[:, a] * keep(2, a)
    for a in range(3):
        for c in range(CHUNKS):
            full_three[c, :, a, own, :] = (
                lower_three[:, a, :, c * WIDTH : (c + 1) * WIDTH] * keep(3, a)
            )
    for part in range(2):
        high, low = split(inverse_root[part])
        chain[0, part, 0, :, :S] = high
        chain[1, part, 0, :, :S] = low

    pl.semaphore_wait(barrier, PROCS - 1 + 3)

    pending = []

    def send(chunk, role, part, proc, to, half=None):
        offset, count = (0, ROWS) if half is None else (half * HALF, HALF)
        rows = pl.ds(rows_of(proc, offset), count)
        parts = slice(None) if part is None else slice(part, part + 1)
        place = buffers[chunk].at[parts, :, rows, :]
        copy = pltpu.make_async_remote_copy(
            src_ref=place,
            dst_ref=place,
            send_sem=gather_send.at[chunk, role],
            recv_sem=gather_recv.at[chunk, role],
            device_id=(group, to),
            device_id_type=MESH,
        )
        copy.start()
        pending.append(copy)

    def arrive(chunk, role, part, proc, half=None):
        offset, count = (0, ROWS) if half is None else (half * HALF, HALF)
        rows = pl.ds(rows_of(proc, offset), count)
        parts = slice(None) if part is None else slice(part, part + 1)
        place = buffers[chunk].at[parts, :, rows, :]
        pltpu.make_async_remote_copy(
            src_ref=place,
            dst_ref=place,
            send_sem=gather_send.at[chunk, role],
            recv_sem=gather_recv.at[chunk, role],
            device_id=(group, sibling),
            device_id_type=MESH,
        ).wait_recv()

    def stage_a(q):
        send(q, 0, 0, me, pair)
        send(q, 9, 1, me, right)
        send(q, 10, 1, me, left)
        send(q, 1, 0, me, right)
        send(q, 2, 0, me, left)
        send(q, 13, 1, me, pair)
        send(q, 17, None, me, sibling)

    def stage_b(q):
        arrive(q, 0, 0, pair)
        send(q, 3, 0, pair, right)
        send(q, 4, 0, pair, left)
        send(q, 18, 0, pair, sibling)
        arrive(q, 9, 1, left)
        send(q, 11, 1, left, right, 0)
        send(q, 14, 1, left, pair)
        send(q, 25, 1, left, sibling)
        arrive(q, 10, 1, right)
        send(q, 12, 1, right, left, 1)
        send(q, 15, 1, right, pair)
        send(q, 26, 1, right, sibling)
        arrive(q, 1, 0, left)
        send(q, 5, 0, left, right, 0)
        send(q, 19, 0, left, sibling)
        arrive(q, 2, 0, right)
        send(q, 6, 0, right, left, 1)
        send(q, 20, 0, right, sibling)

    def stage_c(q):
        arrive(q, 11, 1, far, 0)
        arrive(q, 12, 1, far, 1)
        send(q, 16, 1, far, pair)
        send(q, 27, 1, far, sibling)
        arrive(q, 3, 0, pair_left)
        send(q, 7, 0, pair_left, right, 0)
        send(q, 21, 0, pair_left, sibling)
        arrive(q, 4, 0, pair_right)
        send(q, 8, 0, pair_right, left, 1)
        send(q, 22, 0, pair_right, sibling)

    def stage_d(q):
        arrive(q, 13, 1, pair)
        send(q, 28, 1, pair, sibling)
        arrive(q, 5, 0, far, 0)
        arrive(q, 6, 0, far, 1)
        send(q, 23, 0, far, sibling)
        arrive(q, 14, 1, pair_left)
        send(q, 29, 1, pair_left, sibling)
        arrive(q, 15, 1, pair_right)
        send(q, 30, 1, pair_right, sibling)
        arrive(q, 7, 0, pair_far, 0)
        arrive(q, 8, 0, pair_far, 1)
        send(q, 24, 0, pair_far, sibling)
        arrive(q, 16, 1, pair_far)
        send(q, 31, 1, pair_far, sibling)

    def stage_e(q):
        flip = 1 - 2 * core
        arrive(q, 17, None, sibling)
        for role, part, proc in (
            (18, 0, pair),
            (25, 1, left),
            (26, 1, right),
            (19, 0, left),
            (20, 0, right),
            (27, 1, far),
            (21, 0, pair_left),
            (22, 0, pair_right),
            (28, 1, pair),
            (23, 0, far),
            (29, 1, pair_left),
            (30, 1, pair_right),
            (24, 0, pair_far),
            (31, 1, pair_far),
        ):
            arrive(q, role, part, proc + flip)

    def convert(q):
        for part in range(2):
            for a in range(buffers[q].shape[1]):
                high, low = split(buffers[q][part, a])
                highs[q][part, a] = high
                lows[q][part, a] = low

    def factors(q):
        levels, width = highs[q].shape[1], highs[q].shape[3]
        return [
            ref[part].reshape(levels * S, width) for part in range(2) for ref in (highs[q], lows[q])
        ]

    def new_upper(q, level):
        depth = level * S
        rows = 2 * level * ROWS
        high = chain[0, :, :level, :, :depth].reshape(rows, depth)
        low = chain[1, :, :level, :, :depth].reshape(rows, depth)
        real, imag = complex_rows(high, low, *factors(q))
        shape = (level, ROWS, highs[q].shape[3])
        return -real.reshape(shape), -imag.reshape(shape)

    def join_copies(step, flips, ref, slot):
        copies = []
        for flip in flips:
            copy = pltpu.make_async_remote_copy(
                src_ref=ref.at[slot],
                dst_ref=ref.at[slot],
                send_sem=join_send.at[step, flip],
                recv_sem=join_recv.at[step, flip],
                device_id=(group ^ flip, me),
                device_id_type=MESH,
            )
            copy.start()
            copies.append(copy)
        pending.extend(copies)

    def join_waits(step, flips, ref, slot):
        for flip in flips:
            place = ref.at[slot ^ flip]
            pltpu.make_async_remote_copy(
                src_ref=place,
                dst_ref=place,
                send_sem=join_send.at[step, flip],
                recv_sem=join_recv.at[step, flip],
                device_id=(group ^ flip, me),
                device_id_type=MESH,
            ).wait_recv()

    def widen(pieces):
        lane = lax.broadcasted_iota(jnp.int32, (pieces[0].shape[0], 128), 1)
        tiles = []
        for even, odd in ((pieces[0], pieces[1]), (pieces[2], pieces[3])):
            rolled = pltpu.roll(odd, 64, 1)
            tiles += [
                even[:, :128],
                jnp.where(lane < 64, even[:, 128:], rolled[:, :128]),
                rolled[:, 128:],
            ]
        return jnp.concatenate(tiles, axis=1)

    def window(real, imag, proc, base=0):
        start = proc * ROWS - base
        tile, shift = start // 128 * 128, start % 128
        count = 128 if shift + ROWS <= 128 else 256
        lane = lax.broadcasted_iota(jnp.int32, (real.shape[0], 128), 1)
        first = real[:, tile : tile + count]
        second = imag[:, tile : tile + count]
        if shift:
            first = pltpu.roll(first, count - shift, 1)[:, :128]
        if shift != ROWS:
            second = pltpu.roll(second, (count + ROWS - shift) % count, 1)[:, :128]
        return jnp.where(lane < ROWS, first[:, :128], second[:, :128])

    def turn_copy(level, source, target, to):
        return pltpu.make_async_remote_copy(
            src_ref=source.at[to],
            dst_ref=target.at[:, own, :],
            send_sem=turn_send.at[level - 1, to],
            recv_sem=turn_recv.at[level - 1, me],
            device_id=(group, to),
            device_id_type=MESH,
        )

    def turn_arrive(level, source, target, proc):
        pltpu.make_async_remote_copy(
            src_ref=source.at[proc],
            dst_ref=target.at[:, pl.ds(rows_of(proc), ROWS), :],
            send_sem=turn_send.at[level - 1, proc],
            recv_sem=turn_recv.at[level - 1, proc],
            device_id=(group, proc),
            device_id_type=MESH,
        ).wait_recv()

    def turn_start(level, source, target):
        real = joined[0, :level].reshape(level * ROWS, S)
        imag = joined[1, :level].reshape(level * ROWS, S)
        for proc in range(PROCS):
            source[proc] = window(real, imag, proc).reshape(level, ROWS, 128)
        for step in range(1, PROCS):
            copy = turn_copy(level, source, target, lax.rem(me + step, PROCS))
            copy.start()
            pending.append(copy)
        target[:, own, :] = source[me]

    def turn_finish(level, source, target):
        for step in range(1, PROCS):
            turn_arrive(level, source, target, lax.rem(me + PROCS - step, PROCS))
        flat = target[...].reshape(level * S, 128)
        return split(flat.T[: 2 * ROWS])

    def new_diagonal(q, row_high, row_low):
        return complex_rows(row_high, row_low, *factors(q))

    def put_chain(part, a, columns, value):
        high, low = split(value)
        chain[0, part, a, :, columns] = high
        chain[1, part, a, :, columns] = low

    slot_one, slot_two = lax.rem(group, 4), lax.rem(group, 2)
    flips_one, flips_two = (1, 2, 3), (1,)

    stage_a(0)
    stage_a(1)
    stage_b(0)
    stage_c(0)
    stage_d(0)
    stage_e(0)
    convert(0)
    real, imag = new_upper(0, 1)
    for part, value in ((0, real), (1, imag)):
        upper_one[part] = value[:, :, : COLS[0]]
        join_one[slot_one, part] = value[0]
    join_copies(0, flips_one, join_one, slot_one)
    stage_b(1)
    stage_a(2)
    join_waits(0, flips_one, join_one, slot_one)
    for part in range(2):
        value = widen([join_one[j, part] for j in range(4)])
        joined[part, 0] = value
        put_chain(part, 0, slice(S, 2 * S), value)
    turn_start(1, send_one, turned_one)
    stage_c(1)
    row_high, row_low = turn_finish(1, send_one, turned_one)
    for part in range(2):
        rows = slice(part * ROWS, (part + 1) * ROWS)
        chain[0, part, 1, :, :S] = row_high[rows]
        chain[1, part, 1, :, :S] = row_low[rows]
    product = new_diagonal(0, row_high, row_low)
    for part in range(2):
        value = inverse_one[part] - product[part][:, : COLS[0]]
        diagonal_one[part] = value
        join_diag_one[slot_one, part, :, : COLS[0]] = value
    join_copies(1, flips_one, join_diag_one, slot_one)
    stage_d(1)
    join_waits(1, flips_one, join_diag_one, slot_one)
    for part in range(2):
        value = widen([join_diag_one[j, part] for j in range(4)])
        put_chain(part, 1, slice(S, 2 * S), value)

    stage_e(1)
    convert(1)
    real, imag = new_upper(1, 2)
    for part, value in ((0, real), (1, imag)):
        upper_two[part] = value
        join_two[slot_two, part] = value
    join_copies(2, flips_two, join_two, slot_two)
    stage_b(2)
    stage_a(3)
    join_waits(2, flips_two, join_two, slot_two)
    for part in range(2):
        for j in range(2):
            columns = slice(j * COLS[1], (j + 1) * COLS[1])
            for a in range(2):
                value = join_two[j, part, a]
                joined[part, a, :, columns] = value
                put_chain(part, a, slice(2 * S + j * COLS[1], 2 * S + (j + 1) * COLS[1]), value)
    turn_start(2, send_two, turned_two)
    stage_c(2)
    row_high, row_low = turn_finish(2, send_two, turned_two)
    for part in range(2):
        rows = slice(part * ROWS, (part + 1) * ROWS)
        chain[0, part, 2, :, : 2 * S] = row_high[rows]
        chain[1, part, 2, :, : 2 * S] = row_low[rows]
    product = new_diagonal(1, row_high, row_low)
    for part in range(2):
        value = inverse_two[part] - product[part]
        diagonal_two[part] = value
        join_diag_two[slot_two, part] = value
    join_copies(3, flips_two, join_diag_two, slot_two)
    stage_d(2)
    stage_b(3)
    stage_a(4)
    join_waits(3, flips_two, join_diag_two, slot_two)
    for part in range(2):
        for j in range(2):
            put_chain(
                part,
                2,
                slice(2 * S + j * COLS[1], 2 * S + (j + 1) * COLS[1]),
                join_diag_two[j, part],
            )

    done = 0
    for c in range(CHUNKS):
        q = 2 + c
        if c == 1:
            stage_c(4)
        if c == 2:
            stage_d(4)
        stage_e(q)
        convert(q)
        real, imag = new_upper(q, 3)
        columns = slice(c * WIDTH, (c + 1) * WIDTH)
        for part, value in ((0, real), (1, imag)):
            upper_three[part, :, :, columns] = value
            joined[part, :, :, columns] = value
        ready = (c + 1) * WIDTH // ROWS
        for proc in range(done, ready):
            real = joined[0].reshape(3 * ROWS, S)
            imag = joined[1].reshape(3 * ROWS, S)
            send_three[proc] = window(real, imag, proc).reshape(3, ROWS, 128)

            @pl.when(me != proc)
            def _():
                turn_copy(3, send_three, turned_three, proc).start()

        done = ready
        if c == 0:
            stage_c(3)
            stage_d(3)
            stage_b(4)
    turned_three[:, own, :] = send_three[me]
    row_high, row_low = turn_finish(3, send_three, turned_three)
    for c in range(CHUNKS):
        columns = slice(c * WIDTH, (c + 1) * WIDTH)
        product = new_diagonal(2 + c, row_high, row_low)
        for part in range(2):
            diagonal_three[part, :, columns] = inverse_three[part, :, columns] - product[part]

    for copy in pending:
        copy.wait_send()
    for step in range(1, PROCS):
        turn_copy(3, send_three, turned_three, lax.rem(me + step, PROCS)).wait_send()


def shards(*arguments):
    f32, bf16 = jnp.float32, jnp.bfloat16
    outputs = [jax.ShapeDtypeStruct(a.shape, f32) for a in arguments[5:8] + arguments[2:5]]
    vmem = pl.BlockSpec(memory_space=pltpu.VMEM)
    fulls = [(2, 1, S, WIDE[0]), (2, 2, S, WIDE[1]), (CHUNKS, 2, 3, S, WIDTH)]
    sends = [(PROCS, level, ROWS, 128) for level in (1, 2, 3)]
    turns = [(level, S, 128) for level in (1, 2, 3)]
    return pl.pallas_call(
        kernel,
        out_shape=outputs,
        in_specs=[pl.BlockSpec(memory_space=pltpu.SMEM)] + [vmem] * 7,
        out_specs=[vmem] * 6,
        scratch_shapes=[pltpu.VMEM(shape, f32) for shape in fulls]
        + [pltpu.VMEM(shape, bf16) for shape in fulls]
        + [pltpu.VMEM(shape, bf16) for shape in fulls]
        + [
            pltpu.VMEM((2, 2, 3, ROWS, 3 * S), bf16),
            pltpu.VMEM((4, 2, ROWS, WIDE[0]), f32),
            pltpu.VMEM((2, 2, 2, ROWS, WIDE[1]), f32),
            pltpu.VMEM((2, 3, ROWS, S), f32),
            pltpu.VMEM((4, 2, ROWS, WIDE[0]), f32),
            pltpu.VMEM((2, 2, ROWS, WIDE[1]), f32),
        ]
        + [pltpu.VMEM(shape, f32) for shape in sends]
        + [pltpu.VMEM(shape, f32) for shape in turns]
        + [
            pltpu.SemaphoreType.DMA((2 + CHUNKS, ROLES)),
            pltpu.SemaphoreType.DMA((2 + CHUNKS, ROLES)),
            pltpu.SemaphoreType.DMA((4, 4)),
            pltpu.SemaphoreType.DMA((4, 4)),
            pltpu.SemaphoreType.DMA((3, PROCS)),
            pltpu.SemaphoreType.DMA((3, PROCS)),
        ],
        compiler_params=pltpu.CompilerParams(
            collective_id=0, has_side_effects=True, vmem_limit_bytes=62 * 2**20
        ),
    )(*arguments)


def solution(mesh):
    in_specs = (
        P(),
        P(None, "proc", None),
        P(None, "proc", "group"),
        P(None, "proc", "group"),
        P(None, "proc", "group"),
        P(None, None, "proc", "group"),
        P(None, None, "proc", "group"),
        P(None, None, "proc", "group"),
    )
    out_specs = (
        P(None, None, "proc", "group"),
        P(None, None, "proc", "group"),
        P(None, None, "proc", "group"),
        P(None, "proc", "group"),
        P(None, "proc", "group"),
        P(None, "proc", "group"),
    )
    return jax.shard_map(shards, mesh=mesh, in_specs=in_specs, out_specs=out_specs, check_vma=False)
```

profile of v0, /device:TPU:39, one launch (start us, length us, event | category | flops | bytes accessed | tf_op | source)
XLA Modules:
  0.0 175.7 jit_solution(5904065996118538005)
XLA Ops:
  0.6 167.6 %shard_map.127 = (f32[2,1,48,192]{3,2,1,0:T(8,128)}, f32[2,2,48,384]{3,2,1,0:T(8,128)}, f32[2,3,48,768]{3,2,1,0:T(8,128)}, f32[2,48,192]{2,1,0:T(8,128)}, f32[2,48,384]{2,1,0:T(8,128)}, /*index=5*/f32[2,48,768]{2,1,0:T(8,128)}) custom-call(s32[34]{0:T(128)} %pattern.1, f32[2,48,768]{2,1,0:T(8,128)} %inverse_root.1, f32[2,48,192]{2,1,0:T(8,128)} %inverse_one.1, ...), custom_call_target="tpu_custom_call" | custom-call | tf_op jit(solution)/shard_map/pallas_call | solution.py:497
  168.2 1.5 copy.20
  169.8 1.7 copy.21
  171.5 0.0 copy-start.2
  171.5 0.0 copy-start.1
  171.5 2.2 %copy.22 = f32[2,3,48,768]{3,2,1,0:T(8,128)} copy(f32[2,3,48,768]{3,2,1,0:T(8,128)} %get-tuple-element.14) | data formatting | bytes 1769472
  173.7 0.0 copy-done.2
  173.7 0.0 copy-start
  173.7 0.6 copy.23
  174.3 0.0 copy-done.1
  174.3 0.7 copy.24
  175.0 0.0 copy-done
  175.0 0.7 copy.25
Async XLA Ops:
  171.5 2.2 %copy-start.2 = (f32[2,48,192]{2,1,0:T(8,128)S(1)}, f32[2,48,192]{2,1,0:T(8,128)}, u32[]{:S(2)}) copy-start(f32[2,48,192]{2,1,0:T(8,128)} %get-tuple-element.15) | copy-start | bytes 221188
  171.5 2.8 %copy-start.1 = (f32[2,48,384]{2,1,0:T(8,128)S(1)}, f32[2,48,384]{2,1,0:T(8,128)}, u32[]{:S(2)}) copy-start(f32[2,48,384]{2,1,0:T(8,128)} %get-tuple-element.16) | copy-start | bytes 442372
  173.7 1.3 copy-start
where the time goes:
time: 178 us; the launch traced here: 176 us
  Pallas kernels  168 us (94%)
  local copies, waits for them, and re-layouts  7.44 us (4%)
    pallas_call x1, Pallas kernels, shards(): pl.pallas_call(kernel, out_shape=outputs, in_specs=[pl.BlockSpec(memory_s...  168 us
    unnamed x12, local copies, waits for them, and re-layouts  7.44 us

commit v1 on v0

--- a/solution.py
+++ b/solution.py
@@ -14,7 +14,8 @@
 WIDTH = S // CHUNKS
 WIDE = (256, 384)
 COLS = (192, 384)
-ROLES = 32
+ROLES = 17
+X_FIRST = ((2, 1), (3, 1), (4, 1))
 
 
 def split(value):
@@ -133,113 +134,97 @@
 
     pending = []
 
-    def send(chunk, role, part, proc, to, half=None):
+    def block(chunk, part, proc, half):
         offset, count = (0, ROWS) if half is None else (half * HALF, HALF)
-        rows = pl.ds(rows_of(proc, offset), count)
-        parts = slice(None) if part is None else slice(part, part + 1)
-        place = buffers[chunk].at[parts, :, rows, :]
-        copy = pltpu.make_async_remote_copy(
+        return buffers[chunk].at[part, :, pl.ds(rows_of(proc, offset), count), :]
+
+    def gather_copy(chunk, part, role, proc, to, half):
+        place = block(chunk, part, proc, half)
+        return pltpu.make_async_remote_copy(
             src_ref=place,
             dst_ref=place,
-            send_sem=gather_send.at[chunk, role],
-            recv_sem=gather_recv.at[chunk, role],
+            send_sem=gather_send.at[chunk, part, role],
+            recv_sem=gather_recv.at[chunk, part, role],
             device_id=(group, to),
             device_id_type=MESH,
         )
+
+    def send(chunk, part, role, proc, to, half=None):
+        copy = gather_copy(chunk, part, role, proc, to, half)
         copy.start()
         pending.append(copy)
 
-    def arrive(chunk, role, part, proc, half=None):
-        offset, count = (0, ROWS) if half is None else (half * HALF, HALF)
-        rows = pl.ds(rows_of(proc, offset), count)
-        parts = slice(None) if part is None else slice(part, part + 1)
-        place = buffers[chunk].at[parts, :, rows, :]
-        pltpu.make_async_remote_copy(
-            src_ref=place,
-            dst_ref=place,
-            send_sem=gather_send.at[chunk, role],
-            recv_sem=gather_recv.at[chunk, role],
-            device_id=(group, sibling),
-            device_id_type=MESH,
-        ).wait_recv()
+    def arrive(chunk, part, role, proc, half=None):
+        gather_copy(chunk, part, role, proc, sibling, half).wait_recv()
+
+    def x_first(q, part):
+        return (q, part) in X_FIRST
 
     def stage_a(q):
-        send(q, 0, 0, me, pair)
-        send(q, 9, 1, me, right)
-        send(q, 10, 1, me, left)
-        send(q, 1, 0, me, right)
-        send(q, 2, 0, me, left)
-        send(q, 13, 1, me, pair)
-        send(q, 17, None, me, sibling)
+        for part in range(2):
+            send(q, part, 0, me, pair)
+        for part in range(2):
+            send(q, part, 1, me, right)
+            send(q, part, 2, me, left)
+        for part in range(2):
+            send(q, part, 9, me, sibling)
 
     def stage_b(q):
-        arrive(q, 0, 0, pair)
-        send(q, 3, 0, pair, right)
-        send(q, 4, 0, pair, left)
-        send(q, 18, 0, pair, sibling)
-        arrive(q, 9, 1, left)
-        send(q, 11, 1, left, right, 0)
-        send(q, 14, 1, left, pair)
-        send(q, 25, 1, left, sibling)
-        arrive(q, 10, 1, right)
-        send(q, 12, 1, right, left, 1)
-        send(q, 15, 1, right, pair)
-        send(q, 26, 1, right, sibling)
-        arrive(q, 1, 0, left)
-        send(q, 5, 0, left, right, 0)
-        send(q, 19, 0, left, sibling)
-        arrive(q, 2, 0, right)
-        send(q, 6, 0, right, left, 1)
-        send(q, 20, 0, right, sibling)
+        for part in range(2):
+            if not x_first(q, part):
+                arrive(q, part, 0, pair)
+                send(q, part, 3, pair, right)
+                send(q, part, 4, pair, left)
+                send(q, part, 10, pair, sibling)
+        for part in range(2):
+            arrive(q, part, 1, left)
+            send(q, part, 5, left, right, 0)
+            if x_first(q, part):
+                send(q, part, 3, left, pair)
+            send(q, part, 11, left, sibling)
+            arrive(q, part, 2, right)
+            send(q, part, 6, right, left, 1)
+            if x_first(q, part):
+                send(q, part, 4, right, pair)
+            send(q, part, 12, right, sibling)
 
     def stage_c(q):
-        arrive(q, 11, 1, far, 0)
-        arrive(q, 12, 1, far, 1)
-        send(q, 16, 1, far, pair)
-        send(q, 27, 1, far, sibling)
-        arrive(q, 3, 0, pair_left)
-        send(q, 7, 0, pair_left, right, 0)
-        send(q, 21, 0, pair_left, sibling)
-        arrive(q, 4, 0, pair_right)
-        send(q, 8, 0, pair_right, left, 1)
-        send(q, 22, 0, pair_right, sibling)
+        for part in range(2):
+            arrive(q, part, 5, far, 0)
+            arrive(q, part, 6, far, 1)
+            if x_first(q, part):
+                send(q, part, 7, far, pair)
+                arrive(q, part, 0, pair)
+                send(q, part, 10, pair, sibling)
+            send(q, part, 15, far, sibling)
+        for part in range(2):
+            if not x_first(q, part):
+                arrive(q, part, 3, pair_left)
+                send(q, part, 7, pair_left, right, 0)
+                send(q, part, 13, pair_left, sibling)
+                arrive(q, part, 4, pair_right)
+                send(q, part, 8, pair_right, left, 1)
+                send(q, part, 14, pair_right, sibling)
 
     def stage_d(q):
-        arrive(q, 13, 1, pair)
-        send(q, 28, 1, pair, sibling)
-        arrive(q, 5, 0, far, 0)
-        arrive(q, 6, 0, far, 1)
-        send(q, 23, 0, far, sibling)
-        arrive(q, 14, 1, pair_left)
-        send(q, 29, 1, pair_left, sibling)
-        arrive(q, 15, 1, pair_right)
-        send(q, 30, 1, pair_right, sibling)
-        arrive(q, 7, 0, pair_far, 0)
-        arrive(q, 8, 0, pair_far, 1)
-        send(q, 24, 0, pair_far, sibling)
-        arrive(q, 16, 1, pair_far)
-        send(q, 31, 1, pair_far, sibling)
+        for part in range(2):
+            if x_first(q, part):
+                arrive(q, part, 3, pair_left)
+                send(q, part, 13, pair_left, sibling)
+                arrive(q, part, 4, pair_right)
+                send(q, part, 14, pair_right, sibling)
+                arrive(q, part, 7, pair_far)
+            else:
+                arrive(q, part, 7, pair_far, 0)
+                arrive(q, part, 8, pair_far, 1)
+            send(q, part, 16, pair_far, sibling)
 
     def stage_e(q):
         flip = 1 - 2 * core
-        arrive(q, 17, None, sibling)
-        for role, part, proc in (
-            (18, 0, pair),
-            (25, 1, left),
-            (26, 1, right),
-            (19, 0, left),
-            (20, 0, right),
-            (27, 1, far),
-            (21, 0, pair_left),
-            (22, 0, pair_right),
-            (28, 1, pair),
-            (23, 0, far),
-            (29, 1, pair_left),
-            (30, 1, pair_right),
-            (24, 0, pair_far),
-            (31, 1, pair_far),
-        ):
-            arrive(q, role, part, proc + flip)
+        sources = (me, pair, left, right, pair_left, pair_right, far, pair_far)
+        for part in range(2):
+            for at, proc in enumerate(sources):
+                arrive(q, part, 9 + at, proc + flip)
 
     def convert(q):
         for part in range(2):
@@ -366,7 +351,9 @@
     stage_a(0)
     stage_a(1)
     stage_b(0)
+    stage_a(2)
     stage_c(0)
+    stage_b(1)
     stage_d(0)
     stage_e(0)
     convert(0)
@@ -375,15 +362,17 @@
         upper_one[part] = value[:, :, : COLS[0]]
         join_one[slot_one, part] = value[0]
     join_copies(0, flips_one, join_one, slot_one)
-    stage_b(1)
-    stage_a(2)
+    stage_a(3)
+    stage_c(1)
+    stage_b(2)
     join_waits(0, flips_one, join_one, slot_one)
     for part in range(2):
         value = widen([join_one[j, part] for j in range(4)])
         joined[part, 0] = value
         put_chain(part, 0, slice(S, 2 * S), value)
     turn_start(1, send_one, turned_one)
-    stage_c(1)
+    stage_d(1)
+    stage_a(4)
     row_high, row_low = turn_finish(1, send_one, turned_one)
     for part in range(2):
         rows = slice(part * ROWS, (part + 1) * ROWS)
@@ -395,21 +384,22 @@
         diagonal_one[part] = value
         join_diag_one[slot_one, part, :, : COLS[0]] = value
     join_copies(1, flips_one, join_diag_one, slot_one)
-    stage_d(1)
+    stage_c(2)
+    stage_b(3)
+    stage_e(1)
     join_waits(1, flips_one, join_diag_one, slot_one)
     for part in range(2):
         value = widen([join_diag_one[j, part] for j in range(4)])
         put_chain(part, 1, slice(S, 2 * S), value)
 
-    stage_e(1)
     convert(1)
     real, imag = new_upper(1, 2)
     for part, value in ((0, real), (1, imag)):
         upper_two[part] = value
         join_two[slot_two, part] = value
     join_copies(2, flips_two, join_two, slot_two)
-    stage_b(2)
-    stage_a(3)
+    stage_d(2)
+    stage_c(3)
     join_waits(2, flips_two, join_two, slot_two)
     for part in range(2):
         for j in range(2):
@@ -419,7 +409,8 @@
                 joined[part, a, :, columns] = value
                 put_chain(part, a, slice(2 * S + j * COLS[1], 2 * S + (j + 1) * COLS[1]), value)
     turn_start(2, send_two, turned_two)
-    stage_c(2)
+    stage_b(4)
+    stage_e(2)
     row_high, row_low = turn_finish(2, send_two, turned_two)
     for part in range(2):
         rows = slice(part * ROWS, (part + 1) * ROWS)
@@ -431,9 +422,8 @@
         diagonal_two[part] = value
         join_diag_two[slot_two, part] = value
     join_copies(3, flips_two, join_diag_two, slot_two)
-    stage_d(2)
-    stage_b(3)
-    stage_a(4)
+    stage_d(3)
+    stage_c(4)
     join_waits(3, flips_two, join_diag_two, slot_two)
     for part in range(2):
         for j in range(2):
@@ -448,10 +438,10 @@
     for c in range(CHUNKS):
         q = 2 + c
         if c == 1:
-            stage_c(4)
+            stage_e(3)
         if c == 2:
             stage_d(4)
-        stage_e(q)
+            stage_e(4)
         convert(q)
         real, imag = new_upper(q, 3)
         columns = slice(c * WIDTH, (c + 1) * WIDTH)
@@ -469,10 +459,6 @@
                 turn_copy(3, send_three, turned_three, proc).start()
 
         done = ready
-        if c == 0:
-            stage_c(3)
-            stage_d(3)
-            stage_b(4)
     turned_three[:, own, :] = send_three[me]
     row_high, row_low = turn_finish(3, send_three, turned_three)
     for c in range(CHUNKS):
@@ -485,6 +471,11 @@
         copy.wait_send()
     for step in range(1, PROCS):
         turn_copy(3, send_three, turned_three, lax.rem(me + step, PROCS)).wait_send()
+
+
+def hand_over(*refs):
+    for at in range(6):
+        refs[at + 6][...] = refs[at][...]
 
 
 def shards(*arguments):
@@ -494,7 +485,7 @@
     fulls = [(2, 1, S, WIDE[0]), (2, 2, S, WIDE[1]), (CHUNKS, 2, 3, S, WIDTH)]
     sends = [(PROCS, level, ROWS, 128) for level in (1, 2, 3)]
     turns = [(level, S, 128) for level in (1, 2, 3)]
-    return pl.pallas_call(
+    results = pl.pallas_call(
         kernel,
         out_shape=outputs,
         in_specs=[pl.BlockSpec(memory_space=pltpu.SMEM)] + [vmem] * 7,
@@ -513,8 +504,8 @@
         + [pltpu.VMEM(shape, f32) for shape in sends]
         + [pltpu.VMEM(shape, f32) for shape in turns]
         + [
-            pltpu.SemaphoreType.DMA((2 + CHUNKS, ROLES)),
-            pltpu.SemaphoreType.DMA((2 + CHUNKS, ROLES)),
+            pltpu.SemaphoreType.DMA((2 + CHUNKS, 2, ROLES)),
+            pltpu.SemaphoreType.DMA((2 + CHUNKS, 2, ROLES)),
             pltpu.SemaphoreType.DMA((4, 4)),
             pltpu.SemaphoreType.DMA((4, 4)),
             pltpu.SemaphoreType.DMA((3, PROCS)),
@@ -524,6 +515,12 @@
             collective_id=0, has_side_effects=True, vmem_limit_bytes=62 * 2**20
         ),
     )(*arguments)
+    return pl.pallas_call(
+        hand_over,
+        out_shape=outputs,
+        in_specs=[vmem] * 6,
+        out_specs=[vmem] * 6,
+    )(*results)
 
 
 def solution(mesh):

time: 178 us -> 148 us (0.83); the launches traced: 176 us -> 148 us
  Pallas kernels: 168 us -> 147 us
  local copies, waits for them, and re-layouts: 7.44 us -> 0 us
    pallas_call x1, Pallas kernels: 168 us -> 144 us  [shards(): pl.pallas_call(kernel, out_shape=outputs, in_specs=[pl.BlockSpec(memory_s...]
    unnamed x12 -> x0, local copies, waits for them, and re-layouts: 7.44 us -> none
    pallas_call x0 -> x1, Pallas kernels: none -> 2.7 us  [shards(): pl.pallas_call(hand_over, out_shape=outputs, in_specs=[vmem] * 6, out_spe...]
where the time goes in v1:
time: 148 us
  Pallas kernels  147 us (99%)
    pallas_call x1, Pallas kernels, shards(): pl.pallas_call(kernel, out_shape=outputs, in_specs=[pl.BlockSpec(memory_s...  144 us

profile of v1, /device:TPU:39, one launch (start us, length us, event | category | flops | bytes accessed | tf_op | source)
XLA Modules:
  0.0 147.7 jit_solution(13374265769933953424)
XLA Ops:
  0.6 144.4 %shard_map.127 = (f32[2,1,48,192]{3,2,1,0:T(8,128)}, f32[2,2,48,384]{3,2,1,0:T(8,128)}, f32[2,3,48,768]{3,2,1,0:T(8,128)}, f32[2,48,192]{2,1,0:T(8,128)}, f32[2,48,384]{2,1,0:T(8,128)}, /*index=5*/f32[2,48,768]{2,1,0:T(8,128)}) custom-call(s32[34]{0:T(128)} %pattern.1, f32[2,48,768]{2,1,0:T(8,128)} %inverse_root.1, f32[2,48,192]{2,1,0:T(8,128)} %inverse_one.1, ...), custom_call_target="tpu_custom_call" | custom-call | tf_op jit(solution)/shard_map/pallas_call | solution.py:488
  145.0 2.7 %shard_map.128 = (f32[2,1,48,192]{3,2,1,0:T(8,128)}, f32[2,2,48,384]{3,2,1,0:T(8,128)}, f32[2,3,48,768]{3,2,1,0:T(8,128)}, f32[2,48,192]{2,1,0:T(8,128)}, f32[2,48,384]{2,1,0:T(8,128)}, /*index=5*/f32[2,48,768]{2,1,0:T(8,128)}) custom-call(f32[2,1,48,192]{3,2,1,0:T(8,128)} %get-tuple-element.12.refs_0_, f32[2,2,48,384]{3,2,1,0:T(8,128)} %get-tuple-element.13.refs_1_, ...), custom_call_target="tpu_custom_call" | custom-call | tf_op jit(solution)/shard_map/pallas_call | solution.py:518

commit v2 on v1

--- a/solution.py
+++ b/solution.py
@@ -15,7 +15,7 @@
 WIDE = (256, 384)
 COLS = (192, 384)
 ROLES = 17
-X_FIRST = ((2, 1), (3, 1), (4, 1))
+X_FIRST = ((2, 1), (3, 1))
 
 
 def split(value):
@@ -239,21 +239,21 @@
             ref[part].reshape(levels * S, width) for part in range(2) for ref in (highs[q], lows[q])
         ]
 
-    def new_upper(q, level):
+    def new_upper(q, level, first, last):
         depth = level * S
-        rows = 2 * level * ROWS
-        high = chain[0, :, :level, :, :depth].reshape(rows, depth)
-        low = chain[1, :, :level, :, :depth].reshape(rows, depth)
+        rows = 2 * (last - first) * ROWS
+        high = chain[0, :, first:last, :, :depth].reshape(rows, depth)
+        low = chain[1, :, first:last, :, :depth].reshape(rows, depth)
         real, imag = complex_rows(high, low, *factors(q))
-        shape = (level, ROWS, highs[q].shape[3])
+        shape = (last - first, ROWS, highs[q].shape[3])
         return -real.reshape(shape), -imag.reshape(shape)
 
-    def join_copies(step, flips, ref, slot):
+    def join_copies(step, flips, ref, slot, at=()):
         copies = []
         for flip in flips:
             copy = pltpu.make_async_remote_copy(
-                src_ref=ref.at[slot],
-                dst_ref=ref.at[slot],
+                src_ref=ref.at[(slot, *at)],
+                dst_ref=ref.at[(slot, *at)],
                 send_sem=join_send.at[step, flip],
                 recv_sem=join_recv.at[step, flip],
                 device_id=(group ^ flip, me),
@@ -263,9 +263,9 @@
             copies.append(copy)
         pending.extend(copies)
 
-    def join_waits(step, flips, ref, slot):
+    def join_waits(step, flips, ref, slot, at=()):
         for flip in flips:
-            place = ref.at[slot ^ flip]
+            place = ref.at[(slot ^ flip, *at)]
             pltpu.make_async_remote_copy(
                 src_ref=place,
                 dst_ref=place,
@@ -300,41 +300,49 @@
             second = pltpu.roll(second, (count + ROWS - shift) % count, 1)[:, :128]
         return jnp.where(lane < ROWS, first[:, :128], second[:, :128])
 
-    def turn_copy(level, source, target, to):
+    def turn_copy(turn, source, target, span, to):
         return pltpu.make_async_remote_copy(
-            src_ref=source.at[to],
-            dst_ref=target.at[:, own, :],
-            send_sem=turn_send.at[level - 1, to],
-            recv_sem=turn_recv.at[level - 1, me],
+            src_ref=source.at[to, span],
+            dst_ref=target.at[span, own, :],
+            send_sem=turn_send.at[turn, to],
+            recv_sem=turn_recv.at[turn, me],
             device_id=(group, to),
             device_id_type=MESH,
         )
 
-    def turn_arrive(level, source, target, proc):
+    def turn_arrive(turn, source, target, span, proc):
         pltpu.make_async_remote_copy(
-            src_ref=source.at[proc],
-            dst_ref=target.at[:, pl.ds(rows_of(proc), ROWS), :],
-            send_sem=turn_send.at[level - 1, proc],
-            recv_sem=turn_recv.at[level - 1, proc],
+            src_ref=source.at[proc, span],
+            dst_ref=target.at[span, pl.ds(rows_of(proc), ROWS), :],
+            send_sem=turn_send.at[turn, proc],
+            recv_sem=turn_recv.at[turn, proc],
             device_id=(group, proc),
             device_id_type=MESH,
         ).wait_recv()
 
-    def turn_start(level, source, target):
-        real = joined[0, :level].reshape(level * ROWS, S)
-        imag = joined[1, :level].reshape(level * ROWS, S)
+    def fill(source, first, last, proc):
+        rows = (last - first) * ROWS
+        real = joined[0, first:last].reshape(rows, S)
+        imag = joined[1, first:last].reshape(rows, S)
+        source[proc, first:last] = window(real, imag, proc).reshape(last - first, ROWS, 128)
+
+    def turn_start(turn, source, target, first, last):
+        span = slice(first, last)
         for proc in range(PROCS):
-            source[proc] = window(real, imag, proc).reshape(level, ROWS, 128)
+            fill(source, first, last, proc)
         for step in range(1, PROCS):
-            copy = turn_copy(level, source, target, lax.rem(me + step, PROCS))
+            copy = turn_copy(turn, source, target, span, lax.rem(me + step, PROCS))
             copy.start()
             pending.append(copy)
-        target[:, own, :] = source[me]
-
-    def turn_finish(level, source, target):
+        target[span, own, :] = source[me, span]
+
+    def turn_wait(turn, source, target, first, last):
         for step in range(1, PROCS):
-            turn_arrive(level, source, target, lax.rem(me + PROCS - step, PROCS))
-        flat = target[...].reshape(level * S, 128)
+            proc = lax.rem(me + PROCS - step, PROCS)
+            turn_arrive(turn, source, target, slice(first, last), proc)
+
+    def turned_rows(target):
+        flat = target[...].reshape(target.shape[0] * S, 128)
         return split(flat.T[: 2 * ROWS])
 
     def new_diagonal(q, row_high, row_low):
@@ -357,7 +365,7 @@
     stage_d(0)
     stage_e(0)
     convert(0)
-    real, imag = new_upper(0, 1)
+    real, imag = new_upper(0, 1, 0, 1)
     for part, value in ((0, real), (1, imag)):
         upper_one[part] = value[:, :, : COLS[0]]
         join_one[slot_one, part] = value[0]
@@ -370,10 +378,11 @@
         value = widen([join_one[j, part] for j in range(4)])
         joined[part, 0] = value
         put_chain(part, 0, slice(S, 2 * S), value)
-    turn_start(1, send_one, turned_one)
+    turn_start(0, send_one, turned_one, 0, 1)
     stage_d(1)
     stage_a(4)
-    row_high, row_low = turn_finish(1, send_one, turned_one)
+    turn_wait(0, send_one, turned_one, 0, 1)
+    row_high, row_low = turned_rows(turned_one)
     for part in range(2):
         rows = slice(part * ROWS, (part + 1) * ROWS)
         chain[0, part, 1, :, :S] = row_high[rows]
@@ -387,31 +396,58 @@
     stage_c(2)
     stage_b(3)
     stage_e(1)
+
+    convert(1)
+
+    def upper_two_rows(a):
+        real, imag = new_upper(1, 2, a, a + 1)
+        for part, value in ((0, real), (1, imag)):
+            upper_two[part, a] = value[0]
+            join_two[slot_two, part, a] = value[0]
+        join_copies(2 + a, flips_two, join_two, slot_two, (slice(None), a))
+
+    def join_two_rows(a):
+        join_waits(2 + a, flips_two, join_two, slot_two, (slice(None), a))
+        for part in range(2):
+            for j in range(2):
+                value = join_two[j, part, a]
+                joined[part, a, :, j * COLS[1] : (j + 1) * COLS[1]] = value
+                put_chain(part, a, slice(2 * S + j * COLS[1], 2 * S + (j + 1) * COLS[1]), value)
+        turn_start(1 + a, send_two, turned_two, a, a + 1)
+
+    upper_two_rows(0)
     join_waits(1, flips_one, join_diag_one, slot_one)
     for part in range(2):
         value = widen([join_diag_one[j, part] for j in range(4)])
         put_chain(part, 1, slice(S, 2 * S), value)
-
-    convert(1)
-    real, imag = new_upper(1, 2)
-    for part, value in ((0, real), (1, imag)):
-        upper_two[part] = value
-        join_two[slot_two, part] = value
-    join_copies(2, flips_two, join_two, slot_two)
+    upper_two_rows(1)
+    join_two_rows(0)
     stage_d(2)
     stage_c(3)
-    join_waits(2, flips_two, join_two, slot_two)
-    for part in range(2):
-        for j in range(2):
-            columns = slice(j * COLS[1], (j + 1) * COLS[1])
-            for a in range(2):
-                value = join_two[j, part, a]
-                joined[part, a, :, columns] = value
-                put_chain(part, a, slice(2 * S + j * COLS[1], 2 * S + (j + 1) * COLS[1]), value)
-    turn_start(2, send_two, turned_two)
+    join_two_rows(1)
     stage_b(4)
     stage_e(2)
-    row_high, row_low = turn_finish(2, send_two, turned_two)
+
+    def upper_three_rows(c, first, last):
+        real, imag = new_upper(2 + c, 3, first, last)
+        columns = slice(c * WIDTH, (c + 1) * WIDTH)
+        for part, value in ((0, real), (1, imag)):
+            upper_three[part, first:last, :, columns] = value
+            joined[part, first:last, :, columns] = value
+
+    def turn_three(c):
+        for proc in range(c * WIDTH // ROWS, (c + 1) * WIDTH // ROWS):
+            fill(send_three, 0, 3, proc)
+
+            @pl.when(me != proc)
+            def _():
+                turn_copy(3, send_three, turned_three, slice(0, 3), proc).start()
+
+    convert(2)
+    upper_three_rows(0, 0, 2)
+    for a in range(2):
+        turn_wait(1 + a, send_two, turned_two, a, a + 1)
+    row_high, row_low = turned_rows(turned_two)
     for part in range(2):
         rows = slice(part * ROWS, (part + 1) * ROWS)
         chain[0, part, 2, :, : 2 * S] = row_high[rows]
@@ -421,10 +457,13 @@
         value = inverse_two[part] - product[part]
         diagonal_two[part] = value
         join_diag_two[slot_two, part] = value
-    join_copies(3, flips_two, join_diag_two, slot_two)
+    join_copies(4, flips_two, join_diag_two, slot_two)
     stage_d(3)
     stage_c(4)
-    join_waits(3, flips_two, join_diag_two, slot_two)
+    stage_e(3)
+    convert(3)
+    upper_three_rows(1, 0, 2)
+    join_waits(4, flips_two, join_diag_two, slot_two)
     for part in range(2):
         for j in range(2):
             put_chain(
@@ -433,34 +472,18 @@
                 slice(2 * S + j * COLS[1], 2 * S + (j + 1) * COLS[1]),
                 join_diag_two[j, part],
             )
-
-    done = 0
-    for c in range(CHUNKS):
-        q = 2 + c
-        if c == 1:
-            stage_e(3)
-        if c == 2:
-            stage_d(4)
-            stage_e(4)
-        convert(q)
-        real, imag = new_upper(q, 3)
-        columns = slice(c * WIDTH, (c + 1) * WIDTH)
-        for part, value in ((0, real), (1, imag)):
-            upper_three[part, :, :, columns] = value
-            joined[part, :, :, columns] = value
-        ready = (c + 1) * WIDTH // ROWS
-        for proc in range(done, ready):
-            real = joined[0].reshape(3 * ROWS, S)
-            imag = joined[1].reshape(3 * ROWS, S)
-            send_three[proc] = window(real, imag, proc).reshape(3, ROWS, 128)
-
-            @pl.when(me != proc)
-            def _():
-                turn_copy(3, send_three, turned_three, proc).start()
-
-        done = ready
+    upper_three_rows(0, 2, 3)
+    turn_three(0)
+    stage_d(4)
+    upper_three_rows(1, 2, 3)
+    turn_three(1)
+    stage_e(4)
+    convert(4)
+    upper_three_rows(2, 0, 3)
+    turn_three(2)
     turned_three[:, own, :] = send_three[me]
-    row_high, row_low = turn_finish(3, send_three, turned_three)
+    turn_wait(3, send_three, turned_three, 0, 3)
+    row_high, row_low = turned_rows(turned_three)
     for c in range(CHUNKS):
         columns = slice(c * WIDTH, (c + 1) * WIDTH)
         product = new_diagonal(2 + c, row_high, row_low)
@@ -470,7 +493,8 @@
     for copy in pending:
         copy.wait_send()
     for step in range(1, PROCS):
-        turn_copy(3, send_three, turned_three, lax.rem(me + step, PROCS)).wait_send()
+        to = lax.rem(me + step, PROCS)
+        turn_copy(3, send_three, turned_three, slice(0, 3), to).wait_send()
 
 
 def hand_over(*refs):
@@ -506,10 +530,10 @@
         + [
             pltpu.SemaphoreType.DMA((2 + CHUNKS, 2, ROLES)),
             pltpu.SemaphoreType.DMA((2 + CHUNKS, 2, ROLES)),
-            pltpu.SemaphoreType.DMA((4, 4)),
-            pltpu.SemaphoreType.DMA((4, 4)),
-            pltpu.SemaphoreType.DMA((3, PROCS)),
-            pltpu.SemaphoreType.DMA((3, PROCS)),
+            pltpu.SemaphoreType.DMA((5, 4)),
+            pltpu.SemaphoreType.DMA((5, 4)),
+            pltpu.SemaphoreType.DMA((4, PROCS)),
+            pltpu.SemaphoreType.DMA((4, PROCS)),
         ],
         compiler_params=pltpu.CompilerParams(
             collective_id=0, has_side_effects=True, vmem_limit_bytes=62 * 2**20

time: 148 us -> 141 us (0.953)
  Pallas kernels: 147 us -> 141 us
    pallas_call x1, Pallas kernels: 144 us -> 138 us  [shards(): pl.pallas_call(kernel, out_shape=outputs, in_specs=[pl.BlockSpec(memory_s...]
where the time goes in v2:
time: 141 us
  Pallas kernels  141 us (100%)
    pallas_call x1, Pallas kernels, shards(): pl.pallas_call(kernel, out_shape=outputs, in_specs=[pl.BlockSpec(memory_s...  138 us

profile of v2, /device:TPU:39, one launch (start us, length us, event | category | flops | bytes accessed | tf_op | source)
XLA Modules:
  0.0 141.2 jit_solution(10471944044844749633)
XLA Ops:
  0.6 137.8 %shard_map.127 = (f32[2,1,48,192]{3,2,1,0:T(8,128)}, f32[2,2,48,384]{3,2,1,0:T(8,128)}, f32[2,3,48,768]{3,2,1,0:T(8,128)}, f32[2,48,192]{2,1,0:T(8,128)}, f32[2,48,384]{2,1,0:T(8,128)}, /*index=5*/f32[2,48,768]{2,1,0:T(8,128)}) custom-call(s32[34]{0:T(128)} %pattern.1, f32[2,48,768]{2,1,0:T(8,128)} %inverse_root.1, f32[2,48,192]{2,1,0:T(8,128)} %inverse_one.1, ...), custom_call_target="tpu_custom_call" | custom-call | tf_op jit(solution)/shard_map/pallas_call | solution.py:512
  138.5 2.7 %shard_map.128 = (f32[2,1,48,192]{3,2,1,0:T(8,128)}, f32[2,2,48,384]{3,2,1,0:T(8,128)}, f32[2,3,48,768]{3,2,1,0:T(8,128)}, f32[2,48,192]{2,1,0:T(8,128)}, f32[2,48,384]{2,1,0:T(8,128)}, /*index=5*/f32[2,48,768]{2,1,0:T(8,128)}) custom-call(f32[2,1,48,192]{3,2,1,0:T(8,128)} %get-tuple-element.12.refs_0_, f32[2,2,48,384]{3,2,1,0:T(8,128)} %get-tuple-element.13.refs_1_, ...), custom_call_target="tpu_custom_call" | custom-call | tf_op jit(solution)/shard_map/pallas_call | solution.py:542

commit v3 on v2

--- a/solution.py
+++ b/solution.py
@@ -15,6 +15,7 @@
 WIDE = (256, 384)
 COLS = (192, 384)
 ROLES = 17
+EXTRA = {ROWS: 8, 3 * ROWS: 32}
 X_FIRST = ((2, 1), (3, 1))
 
 
@@ -72,6 +73,9 @@
     send_one,
     send_two,
     send_three,
+    got_one,
+    got_two,
+    got_three,
     turned_one,
     turned_two,
     turned_three,
@@ -116,20 +120,21 @@
         return pl.multiple_of(proc * ROWS + offset, 8)
 
     own = pl.ds(rows_of(me), ROWS)
-    full_one[:, :, own, :] = jnp.zeros((2, 1, ROWS, WIDE[0]), jnp.float32)
-    full_one[:, 0, own, : COLS[0]] = lower_one[:, 0] * keep(1, 0)
-    for a in range(2):
-        full_two[:, a, own, :] = lower_two[:, a] * keep(2, a)
-    for a in range(3):
-        for c in range(CHUNKS):
-            full_three[c, :, a, own, :] = (
-                lower_three[:, a, :, c * WIDTH : (c + 1) * WIDTH] * keep(3, a)
-            )
-    for part in range(2):
-        high, low = split(inverse_root[part])
-        chain[0, part, 0, :, :S] = high
-        chain[1, part, 0, :, :S] = low
-
+
+    def own_block(q):
+        if q == 0:
+            full_one[:, :, own, :] = jnp.zeros((2, 1, ROWS, WIDE[0]), jnp.float32)
+            full_one[:, 0, own, : COLS[0]] = lower_one[:, 0] * keep(1, 0)
+        elif q == 1:
+            for a in range(2):
+                full_two[:, a, own, :] = lower_two[:, a] * keep(2, a)
+        else:
+            columns = slice((q - 2) * WIDTH, (q - 1) * WIDTH)
+            for a in range(3):
+                full_three[q - 2, :, a, own, :] = lower_three[:, a, :, columns] * keep(3, a)
+
+    own_block(0)
+    own_block(1)
     pl.semaphore_wait(barrier, PROCS - 1 + 3)
 
     pending = []
@@ -161,6 +166,8 @@
         return (q, part) in X_FIRST
 
     def stage_a(q):
+        if q > 1:
+            own_block(q)
         for part in range(2):
             send(q, part, 0, me, pair)
         for part in range(2):
@@ -300,20 +307,44 @@
             second = pltpu.roll(second, (count + ROWS - shift) % count, 1)[:, :128]
         return jnp.where(lane < ROWS, first[:, :128], second[:, :128])
 
-    def turn_copy(turn, source, target, span, to):
+    def pack(value):
+        extra = EXTRA[value.shape[0]]
+        kept = value.shape[0] - extra
+        lane = lax.broadcasted_iota(jnp.int32, (extra, 128), 1)
+        spare = value[kept:]
+        parts = [
+            jnp.where(
+                lane < 2 * ROWS,
+                value[t * extra : (t + 1) * extra],
+                pltpu.roll(spare, 2 * ROWS - 32 * t, 1),
+            )
+            for t in range(3)
+        ]
+        return jnp.concatenate(parts + [value[3 * extra : kept]], axis=0)
+
+    def unpack(value, count):
+        extra = EXTRA[count]
+        lane = lax.broadcasted_iota(jnp.int32, (extra, 128), 1)
+        parts = [
+            pltpu.roll(value[t * extra : (t + 1) * extra], 32 * t + 32, 1) for t in range(3)
+        ]
+        spare = jnp.where(lane < 32, parts[0], jnp.where(lane < 64, parts[1], parts[2]))
+        return jnp.concatenate([value, spare], axis=0)
+
+    def turn_copy(turn, source, target, to):
         return pltpu.make_async_remote_copy(
-            src_ref=source.at[to, span],
-            dst_ref=target.at[span, own, :],
+            src_ref=source.at[to],
+            dst_ref=target.at[me],
             send_sem=turn_send.at[turn, to],
             recv_sem=turn_recv.at[turn, me],
             device_id=(group, to),
             device_id_type=MESH,
         )
 
-    def turn_arrive(turn, source, target, span, proc):
+    def turn_arrive(turn, source, target, proc):
         pltpu.make_async_remote_copy(
-            src_ref=source.at[proc, span],
-            dst_ref=target.at[span, pl.ds(rows_of(proc), ROWS), :],
+            src_ref=source.at[proc],
+            dst_ref=target.at[proc],
             send_sem=turn_send.at[turn, proc],
             recv_sem=turn_recv.at[turn, proc],
             device_id=(group, proc),
@@ -324,22 +355,24 @@
         rows = (last - first) * ROWS
         real = joined[0, first:last].reshape(rows, S)
         imag = joined[1, first:last].reshape(rows, S)
-        source[proc, first:last] = window(real, imag, proc).reshape(last - first, ROWS, 128)
+        source[proc] = pack(window(real, imag, proc))
 
     def turn_start(turn, source, target, first, last):
-        span = slice(first, last)
         for proc in range(PROCS):
             fill(source, first, last, proc)
         for step in range(1, PROCS):
-            copy = turn_copy(turn, source, target, span, lax.rem(me + step, PROCS))
+            copy = turn_copy(turn, source, target, lax.rem(me + step, PROCS))
             copy.start()
             pending.append(copy)
-        target[span, own, :] = source[me, span]
-
-    def turn_wait(turn, source, target, first, last):
+        target[me] = source[me]
+
+    def turn_wait(turn, source, target, turned, first, last):
         for step in range(1, PROCS):
-            proc = lax.rem(me + PROCS - step, PROCS)
-            turn_arrive(turn, source, target, slice(first, last), proc)
+            turn_arrive(turn, source, target, lax.rem(me + PROCS - step, PROCS))
+        for proc in range(PROCS):
+            value = unpack(target[proc], (last - first) * ROWS)
+            rows = slice(proc * ROWS, (proc + 1) * ROWS)
+            turned[first:last, rows, :] = value.reshape(last - first, ROWS, 128)
 
     def turned_rows(target):
         flat = target[...].reshape(target.shape[0] * S, 128)
@@ -364,6 +397,10 @@
     stage_b(1)
     stage_d(0)
     stage_e(0)
+    for part in range(2):
+        high, low = split(inverse_root[part])
+        chain[0, part, 0, :, :S] = high
+        chain[1, part, 0, :, :S] = low
     convert(0)
     real, imag = new_upper(0, 1, 0, 1)
     for part, value in ((0, real), (1, imag)):
@@ -378,10 +415,10 @@
         value = widen([join_one[j, part] for j in range(4)])
         joined[part, 0] = value
         put_chain(part, 0, slice(S, 2 * S), value)
-    turn_start(0, send_one, turned_one, 0, 1)
+    turn_start(0, send_one, got_one, 0, 1)
     stage_d(1)
     stage_a(4)
-    turn_wait(0, send_one, turned_one, 0, 1)
+    turn_wait(0, send_one, got_one, turned_one, 0, 1)
     row_high, row_low = turned_rows(turned_one)
     for part in range(2):
         rows = slice(part * ROWS, (part + 1) * ROWS)
@@ -413,7 +450,7 @@
                 value = join_two[j, part, a]
                 joined[part, a, :, j * COLS[1] : (j + 1) * COLS[1]] = value
                 put_chain(part, a, slice(2 * S + j * COLS[1], 2 * S + (j + 1) * COLS[1]), value)
-        turn_start(1 + a, send_two, turned_two, a, a + 1)
+        turn_start(1 + a, send_two.at[a], got_two.at[a], a, a + 1)
 
     upper_two_rows(0)
     join_waits(1, flips_one, join_diag_one, slot_one)
@@ -441,12 +478,12 @@
 
             @pl.when(me != proc)
             def _():
-                turn_copy(3, send_three, turned_three, slice(0, 3), proc).start()
+                turn_copy(3, send_three, got_three, proc).start()
 
     convert(2)
     upper_three_rows(0, 0, 2)
     for a in range(2):
-        turn_wait(1 + a, send_two, turned_two, a, a + 1)
+        turn_wait(1 + a, send_two.at[a], got_two.at[a], turned_two, a, a + 1)
     row_high, row_low = turned_rows(turned_two)
     for part in range(2):
         rows = slice(part * ROWS, (part + 1) * ROWS)
@@ -481,8 +518,8 @@
     convert(4)
     upper_three_rows(2, 0, 3)
     turn_three(2)
-    turned_three[:, own, :] = send_three[me]
-    turn_wait(3, send_three, turned_three, 0, 3)
+    got_three[me] = send_three[me]
+    turn_wait(3, send_three, got_three, turned_three, 0, 3)
     row_high, row_low = turned_rows(turned_three)
     for c in range(CHUNKS):
         columns = slice(c * WIDTH, (c + 1) * WIDTH)
@@ -494,7 +531,7 @@
         copy.wait_send()
     for step in range(1, PROCS):
         to = lax.rem(me + step, PROCS)
-        turn_copy(3, send_three, turned_three, slice(0, 3), to).wait_send()
+        turn_copy(3, send_three, got_three, to).wait_send()
 
 
 def hand_over(*refs):
@@ -507,7 +544,12 @@
     outputs = [jax.ShapeDtypeStruct(a.shape, f32) for a in arguments[5:8] + arguments[2:5]]
     vmem = pl.BlockSpec(memory_space=pltpu.VMEM)
     fulls = [(2, 1, S, WIDE[0]), (2, 2, S, WIDE[1]), (CHUNKS, 2, 3, S, WIDTH)]
-    sends = [(PROCS, level, ROWS, 128) for level in (1, 2, 3)]
+    counts = [level * ROWS - EXTRA[level * ROWS] for level in (1, 3)]
+    sends = [
+        (PROCS, counts[0], 128),
+        (2, PROCS, counts[0], 128),
+        (PROCS, counts[1], 128),
+    ]
     turns = [(level, S, 128) for level in (1, 2, 3)]
     results = pl.pallas_call(
         kernel,
@@ -525,6 +567,7 @@
             pltpu.VMEM((4, 2, ROWS, WIDE[0]), f32),
             pltpu.VMEM((2, 2, ROWS, WIDE[1]), f32),
         ]
+        + [pltpu.VMEM(shape, f32) for shape in sends]
         + [pltpu.VMEM(shape, f32) for shape in sends]
         + [pltpu.VMEM(shape, f32) for shape in turns]
         + [

time: 141 us -> 137 us (0.972)
  Pallas kernels: 141 us -> 137 us
    pallas_call x1, Pallas kernels: 138 us -> 134 us  [shards(): pl.pallas_call(kernel, out_shape=outputs, in_specs=[pl.BlockSpec(memory_s...]
where the time goes in v3:
time: 137 us
  Pallas kernels  137 us (100%)
    pallas_call x1, Pallas kernels, shards(): pl.pallas_call(kernel, out_shape=outputs, in_specs=[pl.BlockSpec(memory_s...  134 us

profile of v3, /device:TPU:39, one launch (start us, length us, event | category | flops | bytes accessed | tf_op | source)
XLA Modules:
  0.0 137.2 jit_solution(15211500852406113784)
XLA Ops:
  0.6 133.8 %shard_map.127 = (f32[2,1,48,192]{3,2,1,0:T(8,128)}, f32[2,2,48,384]{3,2,1,0:T(8,128)}, f32[2,3,48,768]{3,2,1,0:T(8,128)}, f32[2,48,192]{2,1,0:T(8,128)}, f32[2,48,384]{2,1,0:T(8,128)}, /*index=5*/f32[2,48,768]{2,1,0:T(8,128)}) custom-call(s32[34]{0:T(128)} %pattern.1, f32[2,48,768]{2,1,0:T(8,128)} %inverse_root.1, f32[2,48,192]{2,1,0:T(8,128)} %inverse_one.1, ...), custom_call_target="tpu_custom_call" | custom-call | tf_op jit(solution)/shard_map/pallas_call | solution.py:554
  134.5 2.7 %shard_map.128 = (f32[2,1,48,192]{3,2,1,0:T(8,128)}, f32[2,2,48,384]{3,2,1,0:T(8,128)}, f32[2,3,48,768]{3,2,1,0:T(8,128)}, f32[2,48,192]{2,1,0:T(8,128)}, f32[2,48,384]{2,1,0:T(8,128)}, /*index=5*/f32[2,48,768]{2,1,0:T(8,128)}) custom-call(f32[2,1,48,192]{3,2,1,0:T(8,128)} %get-tuple-element.12.refs_0_, f32[2,2,48,384]{3,2,1,0:T(8,128)} %get-tuple-element.13.refs_1_, ...), custom_call_target="tpu_custom_call" | custom-call | tf_op jit(solution)/shard_map/pallas_call | solution.py:585

commit v4 on v3

--- a/solution.py
+++ b/solution.py
@@ -367,11 +367,12 @@
         target[me] = source[me]
 
     def turn_wait(turn, source, target, turned, first, last):
-        for step in range(1, PROCS):
-            turn_arrive(turn, source, target, lax.rem(me + PROCS - step, PROCS))
-        for proc in range(PROCS):
+        for step in range(PROCS):
+            proc = lax.rem(me + PROCS - step, PROCS)
+            if step:
+                turn_arrive(turn, source, target, proc)
             value = unpack(target[proc], (last - first) * ROWS)
-            rows = slice(proc * ROWS, (proc + 1) * ROWS)
+            rows = pl.ds(rows_of(proc), ROWS)
             turned[first:last, rows, :] = value.reshape(last - first, ROWS, 128)
 
     def turned_rows(target):

time: 137 us -> 137 us (level)
  no operation moved by 1% of the time
where the time goes in v4:
time: 137 us
  Pallas kernels  136 us (99%)
    pallas_call x1, Pallas kernels, shards(): pl.pallas_call(kernel, out_shape=outputs, in_specs=[pl.BlockSpec(memory_s...  133 us

profile of v4, /device:TPU:39, one launch (start us, length us, event | category | flops | bytes accessed | tf_op | source)
XLA Modules:
  0.0 136.7 jit_solution(11979531188893125403)
XLA Ops:
  0.6 133.4 %shard_map.127 = (f32[2,1,48,192]{3,2,1,0:T(8,128)}, f32[2,2,48,384]{3,2,1,0:T(8,128)}, f32[2,3,48,768]{3,2,1,0:T(8,128)}, f32[2,48,192]{2,1,0:T(8,128)}, f32[2,48,384]{2,1,0:T(8,128)}, /*index=5*/f32[2,48,768]{2,1,0:T(8,128)}) custom-call(s32[34]{0:T(128)} %pattern.1, f32[2,48,768]{2,1,0:T(8,128)} %inverse_root.1, f32[2,48,192]{2,1,0:T(8,128)} %inverse_one.1, ...), custom_call_target="tpu_custom_call" | custom-call | tf_op jit(solution)/shard_map/pallas_call | solution.py:555
  134.0 2.7 %shard_map.128 = (f32[2,1,48,192]{3,2,1,0:T(8,128)}, f32[2,2,48,384]{3,2,1,0:T(8,128)}, f32[2,3,48,768]{3,2,1,0:T(8,128)}, f32[2,48,192]{2,1,0:T(8,128)}, f32[2,48,384]{2,1,0:T(8,128)}, /*index=5*/f32[2,48,768]{2,1,0:T(8,128)}) custom-call(f32[2,1,48,192]{3,2,1,0:T(8,128)} %get-tuple-element.12.refs_0_, f32[2,2,48,384]{3,2,1,0:T(8,128)} %get-tuple-element.13.refs_1_, ...), custom_call_target="tpu_custom_call" | custom-call | tf_op jit(solution)/shard_map/pallas_call | solution.py:586

commit v5 on v4

--- a/solution.py
+++ b/solution.py
@@ -68,6 +68,7 @@
     join_one,
     join_two,
     joined,
+    padded,
     join_diag_one,
     join_diag_two,
     send_one,
@@ -282,6 +283,17 @@
                 device_id_type=MESH,
             ).wait_recv()
 
+    def squeeze(value):
+        lane = lax.broadcasted_iota(jnp.int32, (HALF, 128), 1)
+        rest = value[:, 128:]
+        rest = jnp.where(lane < 64, rest[:HALF], pltpu.roll(rest[HALF:], 64, 1))
+        return jnp.concatenate([value[:, :128], rest], axis=0)
+
+    def stretch(value):
+        rest = value[ROWS:]
+        rest = jnp.concatenate([rest, pltpu.roll(rest, 64, 1)], axis=0)
+        return jnp.concatenate([value[:ROWS], rest], axis=1)
+
     def widen(pieces):
         lane = lax.broadcasted_iota(jnp.int32, (pieces[0].shape[0], 128), 1)
         tiles = []
@@ -406,14 +418,14 @@
     real, imag = new_upper(0, 1, 0, 1)
     for part, value in ((0, real), (1, imag)):
         upper_one[part] = value[:, :, : COLS[0]]
-        join_one[slot_one, part] = value[0]
+        join_one[slot_one, part] = squeeze(value[0])
     join_copies(0, flips_one, join_one, slot_one)
     stage_a(3)
     stage_c(1)
     stage_b(2)
     join_waits(0, flips_one, join_one, slot_one)
     for part in range(2):
-        value = widen([join_one[j, part] for j in range(4)])
+        value = widen([stretch(join_one[j, part]) for j in range(4)])
         joined[part, 0] = value
         put_chain(part, 0, slice(S, 2 * S), value)
     turn_start(0, send_one, got_one, 0, 1)
@@ -427,9 +439,9 @@
         chain[1, part, 1, :, :S] = row_low[rows]
     product = new_diagonal(0, row_high, row_low)
     for part in range(2):
-        value = inverse_one[part] - product[part][:, : COLS[0]]
-        diagonal_one[part] = value
-        join_diag_one[slot_one, part, :, : COLS[0]] = value
+        diagonal_one[part] = inverse_one[part] - product[part][:, : COLS[0]]
+        padded[:, : COLS[0]] = diagonal_one[part]
+        join_diag_one[slot_one, part] = squeeze(padded[...])
     join_copies(1, flips_one, join_diag_one, slot_one)
     stage_c(2)
     stage_b(3)
@@ -456,7 +468,7 @@
     upper_two_rows(0)
     join_waits(1, flips_one, join_diag_one, slot_one)
     for part in range(2):
-        value = widen([join_diag_one[j, part] for j in range(4)])
+        value = widen([stretch(join_diag_one[j, part]) for j in range(4)])
         put_chain(part, 1, slice(S, 2 * S), value)
     upper_two_rows(1)
     join_two_rows(0)
@@ -562,10 +574,11 @@
         + [pltpu.VMEM(shape, bf16) for shape in fulls]
         + [
             pltpu.VMEM((2, 2, 3, ROWS, 3 * S), bf16),
-            pltpu.VMEM((4, 2, ROWS, WIDE[0]), f32),
+            pltpu.VMEM((4, 2, ROWS + HALF, 128), f32),
             pltpu.VMEM((2, 2, 2, ROWS, WIDE[1]), f32),
             pltpu.VMEM((2, 3, ROWS, S), f32),
-            pltpu.VMEM((4, 2, ROWS, WIDE[0]), f32),
+            pltpu.VMEM((ROWS, WIDE[0]), f32),
+            pltpu.VMEM((4, 2, ROWS + HALF, 128), f32),
             pltpu.VMEM((2, 2, ROWS, WIDE[1]), f32),
         ]
         + [pltpu.VMEM(shape, f32) for shape in sends]

time: 137 us -> 136 us (level)
  no operation moved by 1% of the time
where the time goes in v5:
time: 136 us
  Pallas kernels  135 us (99%)
    pallas_call x1, Pallas kernels, shards(): pl.pallas_call(kernel, out_shape=outputs, in_specs=[pl.BlockSpec(memory_s...  132 us

profile of v5, /device:TPU:39, one launch (start us, length us, event | category | flops | bytes accessed | tf_op | source)
XLA Modules:
  0.0 135.8 jit_solution(11051428625163501281)
XLA Ops:
  0.6 132.5 %shard_map.127 = (f32[2,1,48,192]{3,2,1,0:T(8,128)}, f32[2,2,48,384]{3,2,1,0:T(8,128)}, f32[2,3,48,768]{3,2,1,0:T(8,128)}, f32[2,48,192]{2,1,0:T(8,128)}, f32[2,48,384]{2,1,0:T(8,128)}, /*index=5*/f32[2,48,768]{2,1,0:T(8,128)}) custom-call(s32[34]{0:T(128)} %pattern.1, f32[2,48,768]{2,1,0:T(8,128)} %inverse_root.1, f32[2,48,192]{2,1,0:T(8,128)} %inverse_one.1, ...), custom_call_target="tpu_custom_call" | custom-call | tf_op jit(solution)/shard_map/pallas_call | solution.py:567
  133.1 2.7 %shard_map.128 = (f32[2,1,48,192]{3,2,1,0:T(8,128)}, f32[2,2,48,384]{3,2,1,0:T(8,128)}, f32[2,3,48,768]{3,2,1,0:T(8,128)}, f32[2,48,192]{2,1,0:T(8,128)}, f32[2,48,384]{2,1,0:T(8,128)}, /*index=5*/f32[2,48,768]{2,1,0:T(8,128)}) custom-call(f32[2,1,48,192]{3,2,1,0:T(8,128)} %get-tuple-element.12.refs_0_, f32[2,2,48,384]{3,2,1,0:T(8,128)} %get-tuple-element.13.refs_1_, ...), custom_call_target="tpu_custom_call" | custom-call | tf_op jit(solution)/shard_map/pallas_call | solution.py:599
